TPU v7x, 128 devices: a whole 4x4x4 slice. The times are simulated.
128 devices in a mesh: seq: 64 (over z, y, x), head: 2 (over core).
Axes of the slice: x: 4, y: 4, z: 4, core: 2. Of those that a mesh axis runs over, the one named last changes fastest.
Arguments:
- query_states: bfloat16 [32768, 2048], P('seq', 'head'), may hold values from -4.8125 to 4.8125
- key_states: bfloat16 [32768, 2048], P('seq', 'head'), may hold values from -4.8125 to 4.8125
- value_states: bfloat16 [32768, 2048], P('seq', 'head'), may hold values from -6 to 6
- doc_ids: int32 [64], P('seq'), may hold values from 0 to 15, as said below
- pair_table: int32 [192, 2], P('seq'), may hold values from 0 to 63, as said below
- out_weight: bfloat16 [2048, 4096], P('head'), may hold values from -1 to 1
Outputs:
- projected: bfloat16 [32768, 4096], P(('seq', 'head'))
Inputs may be any that keep to these rules, and one draw needn't show every extreme that they name: `doc_ids`: consecutive from 0 and non-decreasing along the blocks. Every document covers 2 to 8 blocks and lies inside one aligned group of 16 blocks; each group holds four documents: one of 8 blocks, and at least one of 2. `pair_table`: each row holds two blocks a < b of one aligned group of 16 blocks; no row appears twice. In each aligned group exactly 24 rows pair two distinct blocks of one document; which of a document's block pairs are listed is arbitrary, and the others are not listed. The 3 rows of one index of seq hold 1 or 2 same-document rows, in no fixed order; its other rows pair blocks of different documents.
All inputs are finite; a program needn't handle non-finite values.
Results may differ from a plain program's by a relative error of at most 0.0053.
Values may be sent and summed in bfloat16 or wider, within the bound.
A program may use at most 192 MiB of HBM per device.

v0:
```python
import jax
import jax.numpy as jnp
from jax import lax
from jax.sharding import PartitionSpec as P

HD = 128
DOC_MOST = 8


def shifted(block, axis, distance):
    devices = range(lax.axis_size(axis))
    route = [(i - distance, i) for i in devices if i - distance in devices]
    return lax.ppermute(block, axis, route)


def collect_window(stacked):
    ahead_blocks = []
    behind_blocks = []
    for offset in range(1, DOC_MOST):
        ahead_blocks.append(shifted(stacked, "seq", -offset))
        behind_blocks.append(shifted(stacked, "seq", offset))
    return jnp.stack(behind_blocks[::-1] + [stacked] + ahead_blocks, 0)


def local(query_states, key_states, value_states, doc_ids, pair_table, out_weight):
    own_block = lax.axis_index("seq")
    doc_all, pairs_all = (
        lax.all_gather(doc_ids, "seq", axis=0, tiled=True),
        lax.all_gather(pair_table, "seq", axis=0, tiled=True),
    )
    block_rows, columns = query_states.shape
    head_count = columns // HD
    window = collect_window(jnp.stack([key_states, value_states], 0))
    positions = jnp.arange(doc_all.shape[0], dtype=jnp.int32)
    own_doc = doc_all[own_block]
    same_doc = doc_all == own_doc
    length_now = jnp.sum(same_doc.astype(jnp.int32))
    first_block = own_block - jnp.sum((same_doc & (positions < own_block)).astype(jnp.int32))
    query_heads = query_states.reshape(block_rows, head_count, HD)
    score_scale = HD ** (-0.5)

    def visit_tile(step_index, running):
        key_block = first_block + step_index
        low_block = jnp.minimum(key_block, own_block)
        high_block = jnp.maximum(key_block, own_block)
        listed = jnp.any((pairs_all[:, 0] == low_block) & (pairs_all[:, 1] == high_block))
        alive_tile = (key_block == own_block) | listed & (doc_all[key_block] == own_doc)

        def update(current):
            row_max, totals, mixed_sum = current
            window_slot = key_block - own_block + DOC_MOST - 1
            pair_now = lax.dynamic_index_in_dim(window, window_slot, 0, keepdims=False)
            key_heads = pair_now[0].reshape(block_rows, head_count, HD)
            value_heads = pair_now[1].reshape(block_rows, head_count, HD)
            scores = (
                jnp.einsum(
                    "qhd,khd->hqk", query_heads, key_heads, preferred_element_type=jnp.float32
                )
                * score_scale
            )
            new_max = jnp.maximum(row_max, jnp.max(scores, axis=-1))
            shrink = jnp.exp(row_max - new_max)
            weights = jnp.exp(scores - new_max[:, :, None])
            rounded = weights.astype(jnp.bfloat16)
            new_totals = shrink * totals + jnp.sum(weights, axis=-1)
            product = jnp.einsum(
                "hqk,khd->qhd", rounded, value_heads, preferred_element_type=jnp.float32
            )
            new_mixed = shrink.T[:, :, None] * mixed_sum + product
            return (new_max, new_totals, new_mixed)

        def unchanged(current):
            return current

        return lax.cond(alive_tile, update, unchanged, running)

    start_max = jnp.full((head_count, block_rows), -jnp.inf, jnp.float32)
    start_totals = jnp.zeros((head_count, block_rows), jnp.float32)
    start_mixed = jnp.zeros((block_rows, head_count, HD), jnp.float32)
    row_max, totals, mixed_sum = lax.fori_loop(
        0, length_now, visit_tile, (start_max, start_totals, start_mixed)
    )
    attended = (mixed_sum / totals.T[:, :, None]).astype(jnp.bfloat16).reshape(block_rows, columns)
    return lax.psum_scatter(
        jnp.dot(attended, out_weight, preferred_element_type=jnp.float32),
        "head",
        scatter_dimension=0,
        tiled=True,
    ).astype(jnp.bfloat16)


def solution(mesh):
    placed = (
        P("seq", "head"),
        P("seq", "head"),
        P("seq", "head"),
        P("seq"),
        P("seq", None),
        P("head", None),
    )
    return jax.shard_map(
        local, mesh=mesh, in_specs=placed, out_specs=P(("seq", "head"), None), check_vma=False
    )
```

profile of v0, /device:TPU:1, one launch (start us, length us, event | category | flops | bytes accessed | tf_op | source)
XLA Modules:
  0.0 941.9 jit_solution(9076274940553330552)
XLA Ops:
  6.5 1.6 copy.21
  8.1 1.5 copy.20
  9.6 1.5 pad_maximum_fusion
  11.1 7.5 collective-permute-start
  18.7 5.5 collective-permute-start.1
  24.2 3.0 collective-permute-start.2
  27.2 3.8 collective-permute-start.3
  31.0 5.6 collective-permute-start.4
  36.5 25.5 %collective-permute-done = bf16[2,512,1024]{1,2,0:T(8,128)(2,1)} collective-permute-done((bf16[2,512,1024]{1,2,0:T(8,128)(2,1)}, bf16[2,512,1024]{1,2,0:T(8,128)(2,1)}, u32[]{:S(2)}, u32[]{:S(2)}) %collective-permute-start) | collective-permute-done | bytes 2097184 | tf_op jit(solution)/shard_map/ppermute | solution.py:13
  62.0 5.4 collective-permute-start.5
  67.4 61.6 %collective-permute-done.1 = bf16[2,512,1024]{1,2,0:T(8,128)(2,1)} collective-permute-done((bf16[2,512,1024]{1,2,0:T(8,128)(2,1)}, bf16[2,512,1024]{1,2,0:T(8,128)(2,1)}, u32[]{:S(2)}, u32[]{:S(2)}) %collective-permute-start.1) | collective-permute-done | bytes 2097184 | tf_op jit(solution)/shard_map/ppermute | solution.py:13
  129.0 55.7 %collective-permute-start.6 = (bf16[2,512,1024]{1,2,0:T(8,128)(2,1)}, bf16[2,512,1024]{1,2,0:T(8,128)(2,1)}, u32[]{:S(2)}, u32[]{:S(2)}) collective-permute-start(bf16[2,512,1024]{1,2,0:T(8,128)(2,1)} %pad_maximum_fusion), channel_id=1, source_target_pairs={{0,2},{2,4},{4,6},{6,8},{8,10},{10,12},{12,14},{14,16},{16,18},{18... | collective-permute-start | bytes 6291464 | tf_op jit(solution)/shard_map/ppermute | solution.py:13
  184.7 10.3 %collective-permute-done.2 = bf16[2,512,1024]{1,2,0:T(8,128)(2,1)} collective-permute-done((bf16[2,512,1024]{1,2,0:T(8,128)(2,1)}, bf16[2,512,1024]{1,2,0:T(8,128)(2,1)}, u32[]{:S(2)}, u32[]{:S(2)}) %collective-permute-start.2) | collective-permute-done | bytes 2097184 | tf_op jit(solution)/shard_map/ppermute | solution.py:13
  195.0 1.3 collective-permute-start.7
  197.0 0.7 dynamic-slice
  197.6 0.8 dynamic-update-slice
  198.4 196.4 %all-reduce = s32[64]{0:T(128)S(1)} all-reduce(s32[64]{0:T(128)S(1)} %dynamic-update-slice), channel_id=1, replica_groups=mesh['seq'=64,'head'=2] {'seq'}, use_global_device_ids=true, to_apply=%add | all-reduce | flops 64 | bytes 512
  394.8 0.7 dynamic_slice.10
  395.4 1.4 fusion.12
  397.4 1.3 copy.22
  398.7 1.6 copy.23
  400.3 142.1 %all-gather = s32[64,3,2]{1,2,0:T(2,128)S(1)} all-gather(s32[1,3,2]{1,2,0:T(2,128)S(1)} %bitcast.75), channel_id=1, replica_groups=mesh['seq'=64,'head'=2] {'seq'}, dimensions={0}, use_global_device_ids=true | all-gather | bytes 1560 | tf_op jit(solution)/shard_map/all_gather | solution.py:29
  542.4 0.1 reshape.24
  542.5 1.3 collective-permute-start.8
  543.8 1.7 bitcast_dynamic-update-slice_fusion.14
  545.6 1.7 bitcast_dynamic-update-slice_fusion.13
  547.3 1.7 bitcast_dynamic-update-slice_fusion.12
  549.0 1.3 collective-permute-start.9
  550.3 1.7 bitcast_dynamic-update-slice_fusion.11
  552.1 1.3 collective-permute-start.10
  553.4 1.7 bitcast_dynamic-update-slice_fusion.10
  555.1 1.3 collective-permute-start.11
  556.4 1.7 bitcast_dynamic-update-slice_fusion.9
  558.2 1.3 collective-permute-start.12
  559.5 1.7 bitcast_dynamic-update-slice_fusion.8
  561.2 9.9 %collective-permute-done.8 = bf16[2,512,1024]{1,2,0:T(8,128)(2,1)S(1)} collective-permute-done((bf16[2,512,1024]{1,2,0:T(8,128)(2,1)}, bf16[2,512,1024]{1,2,0:T(8,128)(2,1)S(1)}, u32[]{:S(2)}, u32[]{:S(2)}) %collective-permute-start.8) | collective-permute-done | bytes 2097184 | tf_op jit(solution)/shard_map/ppermute | solution.py:13
  571.1 1.3 collective-permute-start.13
  572.4 0.1 bitcast_dynamic-update-slice_fusion.7
  572.6 1.7 bitcast_dynamic-update-slice_fusion.6
  574.3 0.1 bitcast_dynamic-update-slice_fusion.5
  574.5 48.0 %collective-permute-done.9 = bf16[2,512,1024]{1,2,0:T(8,128)(2,1)S(1)} collective-permute-done((bf16[2,512,1024]{1,2,0:T(8,128)(2,1)}, bf16[2,512,1024]{1,2,0:T(8,128)(2,1)S(1)}, u32[]{:S(2)}, u32[]{:S(2)}) %collective-permute-start.9) | collective-permute-done | bytes 2097184 | tf_op jit(solution)/shard_map/ppermute | solution.py:13
  622.5 0.1 bitcast_dynamic-update-slice_fusion.4
  622.6 78.6 %collective-permute-done.10 = bf16[2,512,1024]{1,2,0:T(8,128)(2,1)S(1)} collective-permute-done((bf16[2,512,1024]{1,2,0:T(8,128)(2,1)}, bf16[2,512,1024]{1,2,0:T(8,128)(2,1)S(1)}, u32[]{:S(2)}, u32[]{:S(2)}) %collective-permute-start.10) | collective-permute-done | bytes 2097184 | tf_op jit(solution)/shard_map/ppermute | solution.py:13
  701.3 0.1 bitcast_dynamic-update-slice_fusion.3
  701.4 0.1 bitcast_dynamic-update-slice_fusion.2
  701.6 1.7 bitcast_dynamic-update-slice_fusion.1
  703.3 1.7 bitcast_dynamic-update-slice_fusion
  705.1 0.2 broadcast_in_dim.14
  705.4 10.1 %copy-done = bf16[15,2,512,1024]{2,3,1,0:T(8,128)(2,1)} copy-done((bf16[15,2,512,1024]{2,3,1,0:T(8,128)(2,1)}, bf16[15,2,512,1024]{2,3,1,0:T(8,128)(2,1)S(1)}, u32[]{:S(2)}) %copy-start) | copy-done | bytes 31457304
  715.4 15.9 %while.14 = (s32[]{:T(128)}, f32[8,512]{1,0:T(8,128)S(1)}, f32[8,512]{1,0:T(8,128)S(1)}, f32[512,8,128]{0,2,1:T(8,128)S(1)}, s32[]{:T(128)}, /*index=5*/s32[]{:T...) while((s32[]{:T(128)}, f32[8,512]{1,0:T(8,128)S(1)}, ...), condition=%wide.region_8.9_spmd, body=%wide.region_2.8_spmd.sunk | while | flops 1091580672 | bytes 36964292 | solution.py:80
  716.2 0.7 dynamic_slice.12
  718.2 0.7 and_reduce_fusion.2
  719.6 6.6 conditional.2
  719.7 1.7 constant_dynamic-slice_fusion.1
  721.3 1.3 bitcast_reduce_fusion
  722.7 2.1 bitcast_add_fusion
  724.8 1.4 fusion.2
  727.0 0.7 dynamic_slice.12
  729.0 0.7 and_reduce_fusion.2
  731.3 0.3 divide_convert_fusion
  731.6 10.2 %fusion.13 = f32[512,4096]{1,0:T(8,128)} fusion(bf16[512,1024]{0,1:T(8,128)(2,1)S(1)} %bitcast.72, bf16[1024,4096]{1,0:T(8,128)(2,1)} %param.15), kind=kOutput, calls=%fused_computation.37 | convolution fusion | flops 4294967296 | bytes 17825792 | tf_op jit(solution)/shard_map/dot_general | solution.py:85
  741.8 0.0 reduce-scatter.2.cloned.1.call-update
  741.8 189.4 %reduce-scatter.2.cloned.1.call-done = f32[256,4096]{1,0:T(8,128)} async-done(((f32[512,4096]{1,0:T(8,128)}), f32[256,4096]{1,0:T(8,128)}) %reduce-scatter.2.cloned.1.call-update) | async-done | bytes 4194320 | tf_op jit(solution)/shard_map/reduce_scatter | solution.py:84
  931.3 3.8 convert_element_type.21
  (24 shorter events, 0.1 us)
Async XLA Ops:
  6.5 190.4 %copy-start.3 = (u32[128]{0:T(128)S(1)}, u32[128]{0:T(128)}, u32[]{:S(2)}) copy-start(u32[128]{0:T(128)} %constant.45) | copy-start | bytes 1540
  6.5 390.8 %copy-start.1 = (bf16[512,1024]{1,0:T(8,128)(2,1)S(1)}, bf16[512,1024]{1,0:T(8,128)(2,1)}, u32[]{:S(2)}) copy-start(bf16[512,1024]{1,0:T(8,128)(2,1)} %param.10) | copy-start | bytes 3145732
  6.5 393.8 %copy-start.2 = (s32[3,2]{0,1:T(2,128)S(1)}, s32[3,2]{0,1:T(2,128)}, u32[]{:S(2)}) copy-start(s32[3,2]{0,1:T(2,128)} %param.14) | copy-start | bytes 76
  6.5 924.7 %reduce-scatter.2.cloned.1.call-start = ((), (), s32[]{:S(2)}) async-start(), calls=%async_computation.1 | async-start | bytes 12582912 | tf_op jit(solution)/shard_map/reduce_scatter | solution.py:84
  11.1 50.9 %collective-permute-start = (bf16[2,512,1024]{1,2,0:T(8,128)(2,1)}, bf16[2,512,1024]{1,2,0:T(8,128)(2,1)}, u32[]{:S(2)}, u32[]{:S(2)}) collective-permute-start(bf16[2,512,1024]{1,2,0:T(8,128)(2,1)} %pad_maximum_fusion), channel_id=1, source_target_pairs={{0,14},{2,16},{4,18},{6,20},{8,22},{10,24},{12,26},{14,28},{16,30}... | collective-permute-start | bytes 6291464 | tf_op jit(solution)/shard_map/ppermute | solution.py:13
  18.7 110.3 %collective-permute-start.1 = (bf16[2,512,1024]{1,2,0:T(8,128)(2,1)}, bf16[2,512,1024]{1,2,0:T(8,128)(2,1)}, u32[]{:S(2)}, u32[]{:S(2)}) collective-permute-start(bf16[2,512,1024]{1,2,0:T(8,128)(2,1)} %pad_maximum_fusion), channel_id=1, source_target_pairs={{0,12},{2,14},{4,16},{6,18},{8,20},{10,22},{12,24},{14,26},{16,28}... | collective-permute-start | bytes 6291464 | tf_op jit(solution)/shard_map/ppermute | solution.py:13
  24.2 170.8 %collective-permute-start.2 = (bf16[2,512,1024]{1,2,0:T(8,128)(2,1)}, bf16[2,512,1024]{1,2,0:T(8,128)(2,1)}, u32[]{:S(2)}, u32[]{:S(2)}) collective-permute-start(bf16[2,512,1024]{1,2,0:T(8,128)(2,1)} %pad_maximum_fusion), channel_id=1, source_target_pairs={{0,10},{2,12},{4,14},{6,16},{8,18},{10,20},{12,22},{14,24},{16,26}... | collective-permute-start | bytes 6291464 | tf_op jit(solution)/shard_map/ppermute | solution.py:13
  27.2 515.4 %collective-permute-start.3 = (bf16[2,512,1024]{1,2,0:T(8,128)(2,1)}, bf16[2,512,1024]{1,2,0:T(8,128)(2,1)}, u32[]{:S(2)}, u32[]{:S(2)}) collective-permute-start(bf16[2,512,1024]{1,2,0:T(8,128)(2,1)} %pad_maximum_fusion), channel_id=1, source_target_pairs={{0,8},{2,10},{4,12},{6,14},{8,16},{10,18},{12,20},{14,22},{16,24},... | collective-permute-start | bytes 6291464 | tf_op jit(solution)/shard_map/ppermute | solution.py:13
  31.0 518.1 %collective-permute-start.4 = (bf16[2,512,1024]{1,2,0:T(8,128)(2,1)}, bf16[2,512,1024]{1,2,0:T(8,128)(2,1)}, u32[]{:S(2)}, u32[]{:S(2)}) collective-permute-start(bf16[2,512,1024]{1,2,0:T(8,128)(2,1)} %pad_maximum_fusion), channel_id=1, source_target_pairs={{0,6},{2,8},{4,10},{6,12},{8,14},{10,16},{12,18},{14,20},{16,22},{... | collective-permute-start | bytes 6291464 | tf_op jit(solution)/shard_map/ppermute | solution.py:13
  62.0 490.1 %collective-permute-start.5 = (bf16[2,512,1024]{1,2,0:T(8,128)(2,1)}, bf16[2,512,1024]{1,2,0:T(8,128)(2,1)}, u32[]{:S(2)}, u32[]{:S(2)}) collective-permute-start(bf16[2,512,1024]{1,2,0:T(8,128)(2,1)} %pad_maximum_fusion), channel_id=1, source_target_pairs={{0,4},{2,6},{4,8},{6,10},{8,12},{10,14},{12,16},{14,18},{16,20},{1... | collective-permute-start | bytes 6291464 | tf_op jit(solution)/shard_map/ppermute | solution.py:13
  129.0 426.2 %collective-permute-start.6 = (bf16[2,512,1024]{1,2,0:T(8,128)(2,1)}, bf16[2,512,1024]{1,2,0:T(8,128)(2,1)}, u32[]{:S(2)}, u32[]{:S(2)}) collective-permute-start(bf16[2,512,1024]{1,2,0:T(8,128)(2,1)} %pad_maximum_fusion), channel_id=1, source_target_pairs={{0,2},{2,4},{4,6},{6,8},{8,10},{10,12},{12,14},{14,16},{16,18},{18... | collective-permute-start | bytes 6291464 | tf_op jit(solution)/shard_map/ppermute | solution.py:13
  195.0 363.2 %collective-permute-start.7 = (bf16[2,512,1024]{1,2,0:T(8,128)(2,1)}, bf16[2,512,1024]{1,2,0:T(8,128)(2,1)}, u32[]{:S(2)}, u32[]{:S(2)}) collective-permute-start(bf16[2,512,1024]{1,2,0:T(8,128)(2,1)} %pad_maximum_fusion), channel_id=1, source_target_pairs={{2,0},{4,2},{6,4},{8,6},{10,8},{12,10},{14,12},{16,14},{18,16},{20... | collective-permute-start | bytes 6291464 | tf_op jit(solution)/shard_map/ppermute | solution.py:13
  542.5 28.6 %collective-permute-start.8 = (bf16[2,512,1024]{1,2,0:T(8,128)(2,1)}, bf16[2,512,1024]{1,2,0:T(8,128)(2,1)S(1)}, u32[]{:S(2)}, u32[]{:S(2)}) collective-permute-start(bf16[2,512,1024]{1,2,0:T(8,128)(2,1)} %pad_maximum_fusion), channel_id=1, source_target_pairs={{4,0},{6,2},{8,4},{10,6},{12,8},{14,10},{16,12},{18,14},{20,16},{2... | collective-permute-start | bytes 6291464 | tf_op jit(solution)/shard_map/ppermute | solution.py:13
  549.0 73.5 %collective-permute-start.9 = (bf16[2,512,1024]{1,2,0:T(8,128)(2,1)}, bf16[2,512,1024]{1,2,0:T(8,128)(2,1)S(1)}, u32[]{:S(2)}, u32[]{:S(2)}) collective-permute-start(bf16[2,512,1024]{1,2,0:T(8,128)(2,1)} %pad_maximum_fusion), channel_id=1, source_target_pairs={{6,0},{8,2},{10,4},{12,6},{14,8},{16,10},{18,12},{20,14},{22,16},{... | collective-permute-start | bytes 6291464 | tf_op jit(solution)/shard_map/ppermute | solution.py:13
  552.1 149.2 %collective-permute-start.10 = (bf16[2,512,1024]{1,2,0:T(8,128)(2,1)}, bf16[2,512,1024]{1,2,0:T(8,128)(2,1)S(1)}, u32[]{:S(2)}, u32[]{:S(2)}) collective-permute-start(bf16[2,512,1024]{1,2,0:T(8,128)(2,1)} %pad_maximum_fusion), channel_id=1, source_target_pairs={{8,0},{10,2},{12,4},{14,6},{16,8},{18,10},{20,12},{22,14},{24,16},... | collective-permute-start | bytes 6291464 | tf_op jit(solution)/shard_map/ppermute | solution.py:13
  555.1 146.3 %collective-permute-start.11 = (bf16[2,512,1024]{1,2,0:T(8,128)(2,1)}, bf16[2,512,1024]{1,2,0:T(8,128)(2,1)S(1)}, u32[]{:S(2)}, u32[]{:S(2)}) collective-permute-start(bf16[2,512,1024]{1,2,0:T(8,128)(2,1)} %pad_maximum_fusion), channel_id=1, source_target_pairs={{10,0},{12,2},{14,4},{16,6},{18,8},{20,10},{22,12},{24,14},{26,16}... | collective-permute-start | bytes 6291464 | tf_op jit(solution)/shard_map/ppermute | solution.py:13
  558.2 143.4 %collective-permute-start.12 = (bf16[2,512,1024]{1,2,0:T(8,128)(2,1)}, bf16[2,512,1024]{1,2,0:T(8,128)(2,1)}, u32[]{:S(2)}, u32[]{:S(2)}) collective-permute-start(bf16[2,512,1024]{1,2,0:T(8,128)(2,1)} %pad_maximum_fusion), channel_id=1, source_target_pairs={{12,0},{14,2},{16,4},{18,6},{20,8},{22,10},{24,12},{26,14},{28,16}... | collective-permute-start | bytes 6291464 | tf_op jit(solution)/shard_map/ppermute | solution.py:13
  571.1 132.2 %collective-permute-start.13 = (bf16[2,512,1024]{1,2,0:T(8,128)(2,1)}, bf16[2,512,1024]{1,2,0:T(8,128)(2,1)}, u32[]{:S(2)}, u32[]{:S(2)}) collective-permute-start(bf16[2,512,1024]{1,2,0:T(8,128)(2,1)} %pad_maximum_fusion), channel_id=1, source_target_pairs={{14,0},{16,2},{18,4},{20,6},{22,8},{24,10},{26,12},{28,14},{30,16}... | collective-permute-start | bytes 6291464 | tf_op jit(solution)/shard_map/ppermute | solution.py:13
  705.1 10.4 %copy-start = (bf16[15,2,512,1024]{2,3,1,0:T(8,128)(2,1)}, bf16[15,2,512,1024]{2,3,1,0:T(8,128)(2,1)S(1)}, u32[]{:S(2)}) copy-start(bf16[15,2,512,1024]{2,3,1,0:T(8,128)(2,1)S(1)} %bitcast_dynamic-update-slice_fusion) | copy-start | bytes 94371840
Sparse Core Ops, SparseCore 0:
  742.0 189.2 reduce-scatter.1
where the time goes:
time: 943 us; the launch traced here: 942 us
  waiting for transfers between devices  424 us (45%)
  blocking collectives  338 us (36%)
  starting transfers between devices  95.5 us (10%)
  local copies, waits for them, and re-layouts  39.5 us (4%)
  between operations  14.9 us (2%)
  matrix products  13.6 us (1%)
  other arithmetic  9.96 us (1%)
    ppermute x14, waiting for transfers between devices, shifted(): return lax.ppermute(block, axis, route)  234 us
    unnamed x1, blocking collectives  196 us
    reduce_scatter x1, waiting for transfers between devices, local(): lax.psum_scatter(jnp.dot(attended, out_weight, preferred_element_type=jnp...  189 us
    all_gather x1, blocking collectives, local(): lax.all_gather(pair_table, 'seq', axis=0, tiled=True)  142 us
    ppermute x14, starting transfers between devices, shifted(): return lax.ppermute(block, axis, route)  95.5 us
    unnamed x28, local copies, waits for them, and re-layouts  32.2 us
  transfers between devices with their start and end apart: 15, of which 7 were waited for; matrix products, arithmetic and copies ran while one was open for 2% of the time, Pallas kernels for 0%

commit v1 on v0

v1 whole, which is shorter than its diff:
```python
import functools

import jax
import jax.numpy as jnp
from jax import lax
from jax.experimental import pallas as pl
from jax.experimental.pallas import tpu as pltpu
from jax.sharding import PartitionSpec as P

HD = 128
BLK = 512
GROUP = 16
SIDE = 4
HALF = BLK // 2
TILES = 64
CHUNKS = 2
ROWS = HALF // CHUNKS
COLS = 512
LOG2E = 1.4426950408889634
MESH = pl.DeviceIdType.MESH

K, V, KF, VF, Q, O = 0, 1, 2, 3, 4, 4 + CHUNKS
KINDS = 4 + 2 * CHUNKS


def kernel(
    q_in, k_in, v_in, doc_in, pair_in, w_in, out,
    kbuf, vbuf, state, wbuf, meta, list_v, list_s, stage, *rest,
):
    qbuf, obuf, att = rest[:CHUNKS], rest[CHUNKS : 2 * CHUNKS], rest[2 * CHUNKS : 3 * CHUNKS]
    send_sem, recv_sem, meta_send, meta_recv, far_send, far_recv, w_sem, out_sem, list_sem = rest[3 * CHUNKS :]
    s, c = lax.axis_index("seq"), lax.axis_index("head")
    plane = s // GROUP
    base = plane * GROUP
    p = s - base

    def remote(src, dst, ssem, rsem, seq, core):
        return pltpu.make_async_remote_copy(
            src_ref=src, dst_ref=dst, send_sem=ssem, recv_sem=rsem,
            device_id=(seq, core), device_id_type=MESH,
        )

    def arrived(ref, sem):
        pltpu.make_async_copy(ref, ref, sem).wait()

    barrier = pltpu.get_barrier_semaphore()

    def greet(n, carry):
        pl.semaphore_signal(barrier, inc=1, device_id=(base + (p + n) % GROUP, c), device_id_type=MESH)
        return carry

    def greet_other(n, carry):
        pl.semaphore_signal(barrier, inc=1, device_id=(base + (p + n) % GROUP, 1 - c), device_id_type=MESH)
        return carry

    def greet_far(n, carry):
        pl.semaphore_signal(barrier, inc=1, device_id=((plane + n) % 4 * GROUP + p, c), device_id_type=MESH)
        return carry

    lax.fori_loop(1, GROUP, greet, 0)
    lax.fori_loop(0, GROUP, greet_other, 0)
    lax.fori_loop(1, 4, greet_far, 0)
    lane = lax.broadcasted_iota(jnp.int32, (8, 128), 1)
    row = jnp.where(lane == 0, doc_in[0], 0)
    for r in range(3):
        row = jnp.where(lane == r + 1, pair_in[r, 0] * 64 + pair_in[r, 1], row)
    meta[pl.ds(s, 1)] = row[None]
    pl.semaphore_wait(barrier, 2 * GROUP - 1 + 3)

    def meta_copy(n):
        return remote(
            meta.at[pl.ds(s, 1)], meta.at[pl.ds(s, 1)], meta_send.at[n], meta_recv.at[p],
            base + (p + n) % GROUP, c,
        )

    def far_copy(n):
        rows = pl.ds(base, GROUP)
        return remote(meta.at[rows], meta.at[rows], far_send.at[n], far_recv.at[plane], (plane + n) % 4 * GROUP + p, c)

    lax.fori_loop(1, GROUP, lambda n, x: (meta_copy(n).start(), x)[1], 0)

    def deal(kind, ref, dst, first_row, rows, start):
        def step(n, carry):
            i, j = (n // 2 + p) % 8, n % 2
            seq = base + 8 * c + i
            mine = (seq == s) & (j == c)
            src = ref.at[pl.ds(pl.multiple_of(j * HALF + first_row, 128), rows), pl.ds(pl.multiple_of(i * HD, HD), HD)]
            to = dst(j)

            @pl.when(mine)
            def _():
                if start:
                    pltpu.make_async_copy(src, to, recv_sem.at[kind, p]).start()

            @pl.when(jnp.logical_not(mine))
            def _():
                copy = remote(src, to, send_sem.at[kind, n], recv_sem.at[kind, p], seq, j)
                if start:
                    copy.start()
                else:
                    copy.wait_send()

            return carry

        lax.fori_loop(0, GROUP, step, 0)

    def half_of(buf, b, j):
        return buf.at[b, pl.ds(pl.multiple_of(j * HALF, HALF), HALF)]

    def deal_k(start):
        deal(K, k_in, lambda j: half_of(kbuf, p, j), 0, HALF, start)

    def deal_v(start):
        deal(V, v_in, lambda j: half_of(vbuf, p, j), 0, HALF, start)

    def deal_q(u, start):
        deal(Q + u, q_in, lambda j: qbuf[u].at[p], u * ROWS, ROWS, start)

    deal_k(True)
    deal_v(True)
    for u in range(CHUNKS):
        deal_q(u, True)

    w_rows = pl.ds(pl.multiple_of(c * 1024, 1024), 1024)
    w_other = pl.ds(pl.multiple_of((1 - c) * 1024, 1024), 1024)
    w_own = pltpu.make_async_copy(w_in, wbuf.at[w_rows], w_sem.at[0])
    w_sent = remote(w_in, wbuf.at[w_rows], w_sem.at[1], w_sem.at[2], s, 1 - c)
    w_own.start()
    w_sent.start()

    lax.fori_loop(1, GROUP, lambda n, x: (arrived(meta.at[pl.ds(base + (p + n) % GROUP, 1)], meta_recv.at[(p + n) % GROUP]), x)[1], 0)
    lax.fori_loop(1, 4, lambda n, x: (far_copy(n).start(), x)[1], 0)
    lax.fori_loop(
        1, 4,
        lambda n, x: (arrived(meta.at[pl.ds((plane + n) % 4 * GROUP, GROUP)], far_recv.at[(plane + n) % 4]), x)[1],
        0,
    )

    table = meta[:, 0, :]
    cell = lax.broadcasted_iota(jnp.int32, (64, 256), 1)
    place = lax.broadcasted_iota(jnp.int32, (64, 256), 0)
    qa, ka = cell // GROUP + base, cell % GROUP + base
    code = jnp.minimum(qa, ka) * 64 + jnp.maximum(qa, ka)
    hit = (code == table[:, 1:2]) | (code == table[:, 2:3]) | (code == table[:, 3:4])
    listed = jnp.max(jnp.where(hit, 1.0, 0.0), axis=0, keepdims=True)
    docs = table[:, 0:1]
    doc_q = jnp.sum(jnp.where(place == qa, docs, 0).astype(jnp.float32), axis=0, keepdims=True)
    doc_k = jnp.sum(jnp.where(place == ka, docs, 0).astype(jnp.float32), axis=0, keepdims=True)
    alive = jnp.where((qa[:1] == ka[:1]) | ((listed > 0.5) & (doc_q == doc_k)), 1.0, 0.0)
    upto = jnp.where(
        lax.broadcasted_iota(jnp.int32, (256, 256), 0) <= lax.broadcasted_iota(jnp.int32, (256, 256), 1), 1.0, 0.0
    )
    rank = jnp.dot(
        jnp.broadcast_to(alive, (16, 256)).astype(jnp.bfloat16), upto.astype(jnp.bfloat16),
        preferred_element_type=jnp.float32,
    )[:1]
    pick = jnp.where((alive > 0.5) & (rank == (place + 1).astype(jnp.float32)), 1.0, 0.0)
    cells = jnp.sum(pick * cell.astype(jnp.float32), axis=1, keepdims=True)
    rank_64 = jnp.broadcast_to(rank, (64, 256))
    ends = jnp.sum(jnp.where(cell == place * GROUP + GROUP - 1, rank_64 - 1.0, 0.0), axis=1, keepdims=True)
    opens = jnp.max(
        jnp.where((cell % GROUP == GROUP - 1) & (rank_64 == place.astype(jnp.float32)), 1.0, 0.0), axis=1, keepdims=True
    )
    wide = lax.broadcasted_iota(jnp.int32, (64, 128), 1)
    table_out = jnp.where(wide == 0, cells, jnp.where(wide == 1, opens, jnp.where(wide == 2, ends, 0.0)))
    list_v[...] = table_out.astype(jnp.int32)
    to_scalar = pltpu.make_async_copy(list_v, list_s, list_sem)
    to_scalar.start()
    to_scalar.wait()

    def forward(kind, buf, b):
        return remote(half_of(buf, b, c), half_of(buf, b, c), send_sem.at[kind + 2, b], recv_sem.at[kind + 2, b], s, 1 - c)

    for kind, buf in ((K, kbuf), (V, vbuf)):

        def pass_on(n, carry, kind=kind, buf=buf):
            b = (p + n) % GROUP
            arrived(half_of(buf, b, c), recv_sem.at[kind, b])
            forward(kind, buf, b).start()
            return carry

        lax.fori_loop(0, GROUP, pass_on, 0)

    for kind, buf in ((K, kbuf), (V, vbuf)):

        def landed(b, carry, kind=kind, buf=buf):
            arrived(half_of(buf, b, 1 - c), recv_sem.at[kind + 2, b])
            return carry

        lax.fori_loop(0, GROUP, landed, 0)

    scale = jnp.float32(HD**-0.5 * LOG2E)
    ones = jnp.ones((BLK, HD), jnp.bfloat16)

    def give_back(u, n):
        to = (p + n) % GROUP
        dst = att[u].at[:, pl.ds(pl.multiple_of(p * HD, HD), HD)]
        return remote(obuf[u].at[to], dst, send_sem.at[O + u, n], recv_sem.at[O + u, p], base + to, c)

    def attend(u):
        lax.fori_loop(0, GROUP, lambda b, x: (arrived(qbuf[u].at[b], recv_sem.at[Q + u, b]), x)[1], 0)

        def visit(t, carry):
            top, total = carry
            at = jnp.clip(list_s[t, 0], 0, GROUP * GROUP - 1)
            opened = list_s[t, 1] == 1
            key = at % GROUP
            scores = lax.dot_general(
                qbuf[u][at // GROUP], kbuf[key], (((1,), (1,)), ((), ())), preferred_element_type=jnp.float32
            )
            top = jnp.where(opened, -jnp.inf, top)
            new_top = jnp.maximum(top, jnp.max(scores, axis=1, keepdims=True))
            weights = jnp.exp2((scores - new_top) * scale).astype(jnp.bfloat16)
            shrink = jnp.exp2((top - new_top) * scale)
            values = jnp.concatenate([vbuf[key], ones], axis=1)
            total = shrink * total + jnp.dot(weights, values, preferred_element_type=jnp.float32)
            state[t] = total
            return new_top, total

        start = (jnp.full((ROWS, 1), -jnp.inf, jnp.float32), jnp.zeros((ROWS, 2 * HD), jnp.float32))
        lax.fori_loop(0, TILES, visit, start, unroll=4)

        def finish(b, carry):
            total = state[jnp.clip(list_s[b, 2], 0, TILES - 1)]
            obuf[u][b] = (total[:, :HD] / total[:, HD:]).astype(jnp.bfloat16)
            return carry

        lax.fori_loop(0, GROUP, finish, 0)
        lax.fori_loop(1, GROUP, lambda n, x: (give_back(u, n).start(), x)[1], 0)
        pltpu.make_async_copy(
            obuf[u].at[p], att[u].at[:, pl.ds(pl.multiple_of(p * HD, HD), HD)], recv_sem.at[O + u, p]
        ).start()

    def out_copy(u):
        return pltpu.make_async_copy(stage.at[u], out.at[pl.ds(u * ROWS, ROWS)], out_sem.at[u])

    def project(u):
        lax.fori_loop(
            0, GROUP,
            lambda h, x: (arrived(att[u].at[:, pl.ds(pl.multiple_of(h * HD, HD), HD)], recv_sem.at[O + u, h]), x)[1],
            0,
        )

        def tile(n, carry):
            cols = pl.ds(pl.multiple_of(n * COLS, COLS), COLS)
            stage[u, :, cols] = jnp.dot(att[u][...], wbuf[:, cols], preferred_element_type=jnp.float32).astype(jnp.bfloat16)
            return carry

        lax.fori_loop(0, wbuf.shape[1] // COLS, tile, 0)
        out_copy(u).start()

    for u in range(CHUNKS):
        attend(u)
    w_own.wait()
    w_sent.wait_recv()
    for u in range(CHUNKS):
        project(u)

    lax.fori_loop(1, GROUP, lambda n, x: (meta_copy(n).wait_send(), x)[1], 0)
    lax.fori_loop(1, 4, lambda n, x: (far_copy(n).wait_send(), x)[1], 0)
    deal_k(False)
    deal_v(False)
    for u in range(CHUNKS):
        deal_q(u, False)
        lax.fori_loop(1, GROUP, lambda n, x, u=u: (give_back(u, n).wait_send(), x)[1], 0)
    lax.fori_loop(0, GROUP, lambda b, x: (forward(K, kbuf, b).wait_send(), x)[1], 0)
    lax.fori_loop(0, GROUP, lambda b, x: (forward(V, vbuf, b).wait_send(), x)[1], 0)
    w_sent.wait_send()
    for u in range(CHUNKS):
        out_copy(u).wait()


def local(query_states, key_states, value_states, doc_ids, pair_table, out_weight):
    bf16, dma = jnp.bfloat16, pltpu.SemaphoreType.DMA
    anywhere, scalars = pl.BlockSpec(memory_space=pl.ANY), pl.BlockSpec(memory_space=pltpu.SMEM)
    width = out_weight.shape[1]
    return pl.pallas_call(
        kernel,
        out_shape=jax.ShapeDtypeStruct((HALF, width), bf16),
        in_specs=[anywhere, anywhere, anywhere, scalars, scalars, anywhere],
        out_specs=anywhere,
        scratch_shapes=[
            pltpu.VMEM((GROUP, BLK, HD), bf16),
            pltpu.VMEM((GROUP, BLK, HD), bf16),
            pltpu.VMEM((TILES, ROWS, 2 * HD), jnp.float32),
            pltpu.VMEM((2048, width), bf16),
            pltpu.VMEM((64, 8, 128), jnp.int32),
            pltpu.VMEM((64, 128), jnp.int32),
            pltpu.SMEM((64, 128), jnp.int32),
            pltpu.VMEM((CHUNKS, ROWS, width), bf16),
        ]
        + [pltpu.VMEM((GROUP, ROWS, HD), bf16)] * CHUNKS
        + [pltpu.VMEM((GROUP, ROWS, HD), bf16)] * CHUNKS
        + [pltpu.VMEM((ROWS, 2048), bf16)] * CHUNKS
        + [dma((KINDS, GROUP)), dma((KINDS, GROUP)), dma((GROUP,)), dma((GROUP,)), dma((4,)), dma((4,)),
           dma((3,)), dma((CHUNKS,)), dma],
        compiler_params=pltpu.CompilerParams(
            collective_id=0, has_side_effects=True, vmem_limit_bytes=56 << 20
        ),
    )(query_states, key_states, value_states, doc_ids, pair_table, out_weight)


def solution(mesh):
    placed = (
        P("seq", "head"),
        P("seq", "head"),
        P("seq", "head"),
        P("seq"),
        P("seq", None),
        P("head", None),
    )
    return jax.shard_map(
        local, mesh=mesh, in_specs=placed, out_specs=P(("seq", "head"), None), check_vma=False
    )
```

time: 943 us -> 86.9 us (0.09)
  waiting for transfers between devices: 424 us -> 0 us
  blocking collectives: 338 us -> 0 us
  starting transfers between devices: 95.5 us -> 0 us
  Pallas kernels: 0 us -> 81.6 us
  local copies, waits for them, and re-layouts: 39.5 us -> 4.47 us
  between operations: 14.9 us -> 0.66 us
  matrix products: 13.6 us -> 0 us
  other arithmetic: 9.96 us -> 0 us
    ppermute x14 -> x0, waiting for transfers between devices: 234 us -> none  [shifted(): return lax.ppermute(block, axis, route)]
    unnamed x1 -> x0, blocking collectives: 196 us -> none
    reduce_scatter x1 -> x0, waiting for transfers between devices: 189 us -> none  [local(): lax.psum_scatter(jnp.dot(attended, out_weight, preferred_element_type=jnp...]
    all_gather x1 -> x0, blocking collectives: 142 us -> none  [local(): lax.all_gather(pair_table, 'seq', axis=0, tiled=True)]
    ppermute x14 -> x0, starting transfers between devices: 95.5 us -> none  [shifted(): return lax.ppermute(block, axis, route)]
    pallas_call x0 -> x1, Pallas kernels: none -> 81.6 us  [local(): pl.pallas_call(kernel, out_shape=jax.ShapeDtypeStruct((HALF, width), bf16...]
    unnamed x28 -> x2, local copies, waits for them, and re-layouts: 32.2 us -> 4.47 us
    dot_general x3 -> x0, matrix products: 13.6 us -> none  [the longest x1 10.2 us: local(): jnp.dot(attended, out_weight, preferred_element_type=jnp.float32)]
  transfers between devices with their start and end apart: 15 -> 0, of which waited for: 7 -> 0; matrix products, arithmetic and copies ran while one was open for 2% -> 0% of each run, Pallas kernels for 0% -> 0%
where the time goes in v1:
time: 86.9 us; the launch traced here: 86.7 us
  Pallas kernels  81.6 us (94%)
  local copies, waits for them, and re-layouts  4.47 us (5%)
    pallas_call x1, Pallas kernels, local(): pl.pallas_call(kernel, out_shape=jax.ShapeDtypeStruct((HALF, width), bf16...  81.6 us
    unnamed x2, local copies, waits for them, and re-layouts  4.47 us

profile of v1, /device:TPU:1, one launch (start us, length us, event | category | flops | bytes accessed | tf_op | source)
XLA Modules:
  0.0 86.7 jit_solution(16350095089656967541)
XLA Ops:
  0.7 1.3 %copy.7.pair_in = s32[3,2]{1,0:T(4,128)} copy(s32[3,2]{0,1:T(2,128)} %param.10) | data formatting | bytes 48 | tf_op args[4]
  2.0 81.6 %shard_map.64 = bf16[256,4096]{1,0:T(8,128)(2,1)} custom-call(bf16[512,1024]{1,0:T(8,128)(2,1)} %q_in.1, bf16[512,1024]{1,0:T(8,128)(2,1)} %k_in.1, bf16[512,1024]{1,0:T(8,128)(2,1)} %v_in.1, s32[1]{0:T(128)S(6)} %copy.9.doc_in, s32[3,2]{1,0:T(4,128)} %copy.7.pair_in, bf16[1024,4096]{1,0:T(8,128)(2,1)} %w_in.1), custom_call_target="tpu_custom_call" | custom-call | tf_op jit(solution)/shard_map/pallas_call | solution.py:277
  83.6 3.1 %copy.10 = bf16[256,4096]{1,0:T(8,128)(2,1)} copy(bf16[256,4096]{1,0:T(8,128)(2,1)} %shard_map.64) | data formatting | bytes 4194304

commit v2 on v1

v2 whole, which is shorter than its diff:
```python
import jax
import jax.numpy as jnp
from jax import lax
from jax.experimental import pallas as pl
from jax.experimental.pallas import tpu as pltpu
from jax.sharding import PartitionSpec as P

HD = 128
BLK = 512
GROUP = 16
HALF = BLK // 2
TILES = 64
CHUNKS = 2
ROWS = HALF // CHUNKS
COLS = 512
LOG2E = 1.4426950408889634
MESH = pl.DeviceIdType.MESH

K, V, KF, VF, Q, O = 0, 1, 2, 3, 4, 4 + CHUNKS
KINDS = 4 + 2 * CHUNKS
GATE = False
UNROLL = 16


def kernel(
    q_in, k_in, v_in, doc_in, pair_in, w_in, out,
    kbuf, vbuf, state, wbuf, meta, list_v, list_s, doc_s, pair_s, stage, *rest,
):
    qbuf, obuf, att = rest[:CHUNKS], rest[CHUNKS : 2 * CHUNKS], rest[2 * CHUNKS : 3 * CHUNKS]
    send_sem, recv_sem, block_sem, meta_sem, w_sem, out_sem, own_sem = rest[3 * CHUNKS :]
    s, c = lax.axis_index("seq"), lax.axis_index("head")
    plane = s // GROUP
    base = plane * GROUP
    p = s - base

    def remote(src, dst, ssem, rsem, seq, core):
        return pltpu.make_async_remote_copy(
            src_ref=src, dst_ref=dst, send_sem=ssem, recv_sem=rsem,
            device_id=(seq, core), device_id_type=MESH,
        )

    def arrived(ref, sem):
        pltpu.make_async_copy(ref, ref, sem).wait()

    barrier = pltpu.get_barrier_semaphore()

    def greet(n, carry):
        pl.semaphore_signal(barrier, inc=1, device_id=(base + (p + n) % GROUP, c), device_id_type=MESH)
        pl.semaphore_signal(barrier, inc=1, device_id=(base + (p + n) % GROUP, 1 - c), device_id_type=MESH)
        return carry

    def greet_far(n, carry):
        pl.semaphore_signal(barrier, inc=1, device_id=((plane + n) % 4 * GROUP + p, c), device_id_type=MESH)
        return carry

    lax.fori_loop(1, GROUP, greet, 0)
    lax.fori_loop(1, 4, greet_far, 0)
    pl.semaphore_signal(barrier, inc=1, device_id=(s, 1 - c), device_id_type=MESH)

    w_rows = pl.ds(pl.multiple_of(c * 1024, 1024), 1024)
    w_own = pltpu.make_async_copy(w_in, wbuf.at[w_rows], w_sem.at[0])
    w_own.start()
    doc_copy = pltpu.make_async_copy(doc_in, doc_s, own_sem.at[0])
    pair_copy = pltpu.make_async_copy(pair_in, pair_s, own_sem.at[1])
    doc_copy.start()
    pair_copy.start()
    doc_copy.wait()
    pair_copy.wait()
    lane = lax.broadcasted_iota(jnp.int32, (8, 128), 1)
    row = jnp.where(lane == 0, doc_s[0], 0)
    for r in range(3):
        row = jnp.where(lane == r + 1, pair_s[r, 0] * 64 + pair_s[r, 1], row)
    meta[pl.ds(s, 1)] = row[None]
    pl.semaphore_wait(barrier, 2 * GROUP - 1 + 3)

    def meta_copy(n, carry):
        own = meta.at[pl.ds(s, 1)]
        remote(own, own, meta_sem.at[0], meta_sem.at[1], base + (p + n) % GROUP, c).start()
        return carry

    def far_copy(n, carry):
        rows = meta.at[pl.ds(base, GROUP)]
        remote(rows, rows, meta_sem.at[2], meta_sem.at[3], (plane + n) % 4 * GROUP + p, c).start()
        return carry

    lax.fori_loop(1, GROUP, meta_copy, 0)

    def deal(kind, ref, dst, recv, first_row, rows):
        def step(n, carry):
            i = (n + p) % 8
            seq = base + 8 * c + i
            for j in range(2):
                src = ref.at[pl.ds(j * HALF + first_row, rows), pl.ds(pl.multiple_of(i * HD, HD), HD)]
                mine = (seq == s) & (c == j)

                @pl.when(mine)
                def _(src=src, j=j):
                    pltpu.make_async_copy(src, dst(j), recv).start()

                @pl.when(jnp.logical_not(mine))
                def _(src=src, j=j):
                    remote(src, dst(j), send_sem.at[kind], recv, seq, j).start()

            return carry

        lax.fori_loop(0, 8, step, 0)

    def dealt(kind, rows):
        own = p // 8 == c

        @pl.when(own)
        def _():
            arrived(kbuf.at[pl.ds(0, GROUP - 1), pl.ds(0, rows)], send_sem.at[kind])

        @pl.when(jnp.logical_not(own))
        def _():
            arrived(kbuf.at[:, pl.ds(0, rows)], send_sem.at[kind])

    def half_of(buf, b, j):
        return buf.at[b, pl.ds(pl.multiple_of(j * HALF, HALF), HALF)]

    def deal_q(u):
        deal(Q + u, q_in, lambda j: qbuf[u].at[p], recv_sem.at[Q + u], u * ROWS, ROWS)

    deal(K, k_in, lambda j: half_of(kbuf, p, j), block_sem.at[K, p], 0, HALF)
    deal(V, v_in, lambda j: half_of(vbuf, p, j), block_sem.at[V, p], 0, HALF)
    w_sent = remote(w_in, wbuf.at[w_rows], w_sem.at[1], w_sem.at[2], s, 1 - c)
    w_sent.start()
    if not GATE:
        for u in range(CHUNKS):
            deal_q(u)

    arrived(meta.at[pl.ds(0, GROUP - 1)], meta_sem.at[1])
    lax.fori_loop(1, 4, far_copy, 0)
    arrived(meta.at[pl.ds(0, 3 * GROUP)], meta_sem.at[3])

    table = meta[:, 0, :]
    cell = lax.broadcasted_iota(jnp.int32, (64, 256), 1)
    place = lax.broadcasted_iota(jnp.int32, (64, 256), 0)
    qa, ka = cell // GROUP + base, cell % GROUP + base
    code = jnp.minimum(qa, ka) * 64 + jnp.maximum(qa, ka)
    hit = (code == table[:, 1:2]) | (code == table[:, 2:3]) | (code == table[:, 3:4])
    listed = jnp.max(jnp.where(hit, 1.0, 0.0), axis=0, keepdims=True)
    docs = table[:, 0:1]
    doc_q = jnp.sum(jnp.where(place == qa, docs, 0).astype(jnp.float32), axis=0, keepdims=True)
    doc_k = jnp.sum(jnp.where(place == ka, docs, 0).astype(jnp.float32), axis=0, keepdims=True)
    alive = jnp.where((qa[:1] == ka[:1]) | ((listed > 0.5) & (doc_q == doc_k)), 1.0, 0.0)
    upto = jnp.where(
        lax.broadcasted_iota(jnp.int32, (256, 256), 0) <= lax.broadcasted_iota(jnp.int32, (256, 256), 1), 1.0, 0.0
    )
    rank = jnp.dot(
        jnp.broadcast_to(alive, (16, 256)).astype(jnp.bfloat16), upto.astype(jnp.bfloat16),
        preferred_element_type=jnp.float32,
    )[:1]
    pick = jnp.where((alive > 0.5) & (rank == (place + 1).astype(jnp.float32)), 1.0, 0.0)
    cells = jnp.sum(pick * cell.astype(jnp.float32), axis=1, keepdims=True)
    rank_64 = jnp.broadcast_to(rank, (64, 256))
    ends = jnp.sum(jnp.where(cell == place * GROUP + GROUP - 1, rank_64 - 1.0, 0.0), axis=1, keepdims=True)
    opens = jnp.max(
        jnp.where((cell % GROUP == GROUP - 1) & (rank_64 == place.astype(jnp.float32)), 1.0, 0.0), axis=1, keepdims=True
    )
    wide = lax.broadcasted_iota(jnp.int32, (64, 128), 1)
    table_out = jnp.where(wide == 0, cells, jnp.where(wide == 1, opens, jnp.where(wide == 2, ends, 0.0)))
    list_v[...] = table_out.astype(jnp.int32)
    to_scalar = pltpu.make_async_copy(list_v, list_s, own_sem.at[0])
    to_scalar.start()
    to_scalar.wait()

    def pass_all(kind, buf):
        def pass_on(n, carry):
            b = (p + n) % GROUP
            part = half_of(buf, b, c)
            arrived(part, block_sem.at[kind, b])
            remote(part, part, send_sem.at[kind + 2], recv_sem.at[kind + 2], s, 1 - c).start()
            return carry

        lax.fori_loop(0, GROUP, pass_on, 0)

    pass_all(K, kbuf)
    if GATE:
        dealt(K, HALF)
        deal_q(0)
    pass_all(V, vbuf)
    if GATE:
        dealt(V, HALF)
        for u in range(1, CHUNKS):
            deal_q(u)
    other = pl.ds(pl.multiple_of((1 - c) * HALF, HALF), HALF)
    arrived(kbuf.at[:, other], recv_sem.at[KF])
    arrived(vbuf.at[:, other], recv_sem.at[VF])
    if not GATE:
        dealt(K, HALF)
        dealt(V, HALF)
    arrived(meta.at[pl.ds(0, GROUP - 1)], meta_sem.at[0])
    arrived(meta.at[pl.ds(0, 3 * GROUP)], meta_sem.at[2])
    arrived(kbuf.at[:, other], send_sem.at[KF])

    scale = jnp.float32(HD**-0.5 * LOG2E)
    ones = jnp.ones((BLK, HD), jnp.bfloat16)
    columns = pl.ds(pl.multiple_of(p * HD, HD), HD)

    def attend(u):
        arrived(qbuf[u], recv_sem.at[Q + u])

        def visit(t, carry):
            top, total = carry
            at = jnp.clip(list_s[t, 0], 0, GROUP * GROUP - 1)
            opened = list_s[t, 1] == 1
            key = at % GROUP
            scores = lax.dot_general(
                qbuf[u][at // GROUP], kbuf[key], (((1,), (1,)), ((), ())), preferred_element_type=jnp.float32
            )
            top = jnp.where(opened, -jnp.inf, top)
            new_top = jnp.maximum(top, jnp.max(scores, axis=1, keepdims=True))
            weights = jnp.exp2((scores - new_top) * scale).astype(jnp.bfloat16)
            shrink = jnp.exp2((top - new_top) * scale)
            values = jnp.concatenate([vbuf[key], ones], axis=1)
            total = shrink * total + jnp.dot(weights, values, preferred_element_type=jnp.float32)
            state[t] = total
            return new_top, total

        start = (jnp.full((ROWS, 1), -jnp.inf, jnp.float32), jnp.zeros((ROWS, 2 * HD), jnp.float32))
        lax.fori_loop(0, TILES, visit, start, unroll=UNROLL)

        def finish(n, carry):
            b = (p + n) % GROUP
            total = state[jnp.clip(list_s[b, 2], 0, TILES - 1)]
            obuf[u][b] = (total[:, :HD] / total[:, HD:]).astype(jnp.bfloat16)
            remote(obuf[u].at[b], att[u].at[:, columns], send_sem.at[O + u], recv_sem.at[O + u], base + b, c).start()
            return carry

        lax.fori_loop(1, GROUP, finish, 0)
        total = state[jnp.clip(list_s[p, 2], 0, TILES - 1)]
        obuf[u][p] = (total[:, :HD] / total[:, HD:]).astype(jnp.bfloat16)
        pltpu.make_async_copy(obuf[u].at[p], att[u].at[:, columns], recv_sem.at[O + u]).start()

    def out_copy(u):
        return pltpu.make_async_copy(stage.at[u], out.at[pl.ds(u * ROWS, ROWS)], out_sem.at[u])

    def project(u):
        arrived(att[u], recv_sem.at[O + u])

        def tile(n, carry):
            cols = pl.ds(pl.multiple_of(n * COLS, COLS), COLS)
            stage[u, :, cols] = jnp.dot(att[u][...], wbuf[:, cols], preferred_element_type=jnp.float32).astype(jnp.bfloat16)
            return carry

        lax.fori_loop(0, wbuf.shape[1] // COLS, tile, 0)
        out_copy(u).start()

    for u in range(CHUNKS):
        attend(u)
    w_own.wait()
    w_sent.wait()
    arrived(vbuf.at[:, other], send_sem.at[VF])
    for u in range(CHUNKS):
        dealt(Q + u, ROWS)
    for u in range(CHUNKS):
        project(u)
    for u in range(CHUNKS):
        arrived(obuf[u].at[pl.ds(0, GROUP - 1)], send_sem.at[O + u])
    for u in range(CHUNKS):
        out_copy(u).wait()


def local(query_states, key_states, value_states, doc_ids, pair_table, out_weight):
    bf16, dma = jnp.bfloat16, pltpu.SemaphoreType.DMA
    anywhere = pl.BlockSpec(memory_space=pl.ANY)
    width = out_weight.shape[1]
    return pl.pallas_call(
        kernel,
        out_shape=jax.ShapeDtypeStruct((HALF, width), bf16),
        in_specs=[anywhere] * 6,
        out_specs=anywhere,
        scratch_shapes=[
            pltpu.VMEM((GROUP, BLK, HD), bf16),
            pltpu.VMEM((GROUP, BLK, HD), bf16),
            pltpu.VMEM((TILES, ROWS, 2 * HD), jnp.float32),
            pltpu.VMEM((2048, width), bf16),
            pltpu.VMEM((64, 8, 128), jnp.int32),
            pltpu.VMEM((64, 128), jnp.int32),
            pltpu.SMEM((64, 128), jnp.int32),
            pltpu.SMEM((1,), jnp.int32),
            pltpu.SMEM((3, 2), jnp.int32),
            pltpu.VMEM((CHUNKS, ROWS, width), bf16),
        ]
        + [pltpu.VMEM((GROUP, ROWS, HD), bf16)] * CHUNKS
        + [pltpu.VMEM((GROUP, ROWS, HD), bf16)] * CHUNKS
        + [pltpu.VMEM((ROWS, 2048), bf16)] * CHUNKS
        + [dma((KINDS,)), dma((KINDS,)), dma((2, GROUP)), dma((4,)), dma((3,)), dma((CHUNKS,)), dma((2,))],
        compiler_params=pltpu.CompilerParams(
            collective_id=0, has_side_effects=True, vmem_limit_bytes=56 << 20
        ),
    )(query_states, key_states, value_states, doc_ids, pair_table, out_weight)


def solution(mesh):
    placed = (
        P("seq", "head"),
        P("seq", "head"),
        P("seq", "head"),
        P("seq"),
        P("seq", None),
        P("head", None),
    )
    return jax.shard_map(
        local, mesh=mesh, in_specs=placed, out_specs=P(("seq", "head"), None), check_vma=False
    )
```

time: 86.9 us -> 73.1 us (0.84)
  Pallas kernels: 81.6 us -> 67.8 us
    pallas_call x1, Pallas kernels: 81.6 us -> 67.8 us  [local(): pl.pallas_call(kernel, out_shape=jax.ShapeDtypeStruct((HALF, width), bf16...]
where the time goes in v2:
time: 73.1 us; the launch traced here: 72.9 us
  Pallas kernels  67.8 us (93%)
  local copies, waits for them, and re-layouts  4.47 us (6%)
    pallas_call x1, Pallas kernels, local(): pl.pallas_call(kernel, out_shape=jax.ShapeDtypeStruct((HALF, width), bf16...  67.8 us
    unnamed x2, local copies, waits for them, and re-layouts  4.47 us

profile of v2, /device:TPU:1, one launch (start us, length us, event | category | flops | bytes accessed | tf_op | source)
XLA Modules:
  0.0 72.9 jit_solution(9833680817649692911)
XLA Ops:
  0.7 1.3 %copy.7.pair_in = s32[3,2]{1,0:T(4,128)} copy(s32[3,2]{0,1:T(2,128)} %param.10) | data formatting | bytes 48 | tf_op args[4]
  2.0 67.8 %shard_map.64 = bf16[256,4096]{1,0:T(8,128)(2,1)} custom-call(bf16[512,1024]{1,0:T(8,128)(2,1)} %q_in.1, bf16[512,1024]{1,0:T(8,128)(2,1)} %k_in.1, bf16[512,1024]{1,0:T(8,128)(2,1)} %v_in.1, s32[1]{0:T(128)S(6)} %copy.9.doc_in, s32[3,2]{1,0:T(4,128)} %copy.7.pair_in, bf16[1024,4096]{1,0:T(8,128)(2,1)} %w_in.1), custom_call_target="tpu_custom_call" | custom-call | tf_op jit(solution)/shard_map/pallas_call | solution.py:270
  69.8 3.1 %copy.10 = bf16[256,4096]{1,0:T(8,128)(2,1)} copy(bf16[256,4096]{1,0:T(8,128)(2,1)} %shard_map.64) | data formatting | bytes 4194304

commit v3 on v2

--- a/solution.py
+++ b/solution.py
@@ -1,3 +1,5 @@
+import functools
+
 import jax
 import jax.numpy as jnp
 from jax import lax
@@ -10,24 +12,28 @@
 GROUP = 16
 HALF = BLK // 2
 TILES = 64
-CHUNKS = 2
-ROWS = HALF // CHUNKS
+SIZES = (128, 128)
+FIRSTS = (0, 128)
+STEPS = ((0, 32, 0, 4), (32, 48, 4, 8), (48, 64, 8, 16))
+PROJ_UNROLL = 4
+STEP_X = sum(d << 2 * n for n, d in enumerate((2, 2, 1, 3, 1, 3, 0, 0)))
+STEP_Y = sum(d << 2 * n for n, d in enumerate((1, 0, 1, 1, 0, 0, 1, 0)))
+CHUNKS = len(SIZES)
+MOST = max(SIZES)
 COLS = 512
 LOG2E = 1.4426950408889634
 MESH = pl.DeviceIdType.MESH
 
 K, V, KF, VF, Q, O = 0, 1, 2, 3, 4, 4 + CHUNKS
 KINDS = 4 + 2 * CHUNKS
-GATE = False
-UNROLL = 16
 
 
 def kernel(
     q_in, k_in, v_in, doc_in, pair_in, w_in, out,
-    kbuf, vbuf, state, wbuf, meta, list_v, list_s, doc_s, pair_s, stage, *rest,
+    kbuf, vbuf, state, wbuf, meta, list_v, list_s, doc_s, pair_s, *rest,
 ):
-    qbuf, obuf, att = rest[:CHUNKS], rest[CHUNKS : 2 * CHUNKS], rest[2 * CHUNKS : 3 * CHUNKS]
-    send_sem, recv_sem, block_sem, meta_sem, w_sem, out_sem, own_sem = rest[3 * CHUNKS :]
+    qbuf, obuf = rest[:CHUNKS], rest[CHUNKS : 2 * CHUNKS]
+    att, partial_sum, send_sem, recv_sem, back_sem, block_sem, meta_sem, w_sem, own_sem = rest[2 * CHUNKS :]
     s, c = lax.axis_index("seq"), lax.axis_index("head")
     plane = s // GROUP
     base = plane * GROUP
@@ -41,6 +47,12 @@
 
     def arrived(ref, sem):
         pltpu.make_async_copy(ref, ref, sem).wait()
+
+    x, y = p % 4, p // 4
+
+    def block_at(place):
+        step = place // 2 * 2
+        return (y + (STEP_Y >> step & 3) + place % 2 * 2) % 4 * 4 + (x + (STEP_X >> step & 3)) % 4
 
     barrier = pltpu.get_barrier_semaphore()
 
@@ -69,7 +81,7 @@
     lane = lax.broadcasted_iota(jnp.int32, (8, 128), 1)
     row = jnp.where(lane == 0, doc_s[0], 0)
     for r in range(3):
-        row = jnp.where(lane == r + 1, pair_s[r, 0] * 64 + pair_s[r, 1], row)
+        row = jnp.where(lane == r + 1, pair_s[0, r] * 64 + pair_s[1, r], row)
     meta[pl.ds(s, 1)] = row[None]
     pl.semaphore_wait(barrier, 2 * GROUP - 1 + 3)
 
@@ -120,15 +132,13 @@
         return buf.at[b, pl.ds(pl.multiple_of(j * HALF, HALF), HALF)]
 
     def deal_q(u):
-        deal(Q + u, q_in, lambda j: qbuf[u].at[p], recv_sem.at[Q + u], u * ROWS, ROWS)
+        deal(Q + u, q_in, lambda j: qbuf[u].at[p], recv_sem.at[Q + u], FIRSTS[u], SIZES[u])
 
     deal(K, k_in, lambda j: half_of(kbuf, p, j), block_sem.at[K, p], 0, HALF)
     deal(V, v_in, lambda j: half_of(vbuf, p, j), block_sem.at[V, p], 0, HALF)
     w_sent = remote(w_in, wbuf.at[w_rows], w_sem.at[1], w_sem.at[2], s, 1 - c)
     w_sent.start()
-    if not GATE:
-        for u in range(CHUNKS):
-            deal_q(u)
+    deal_q(0)
 
     arrived(meta.at[pl.ds(0, GROUP - 1)], meta_sem.at[1])
     lax.fori_loop(1, 4, far_copy, 0)
@@ -137,7 +147,8 @@
     table = meta[:, 0, :]
     cell = lax.broadcasted_iota(jnp.int32, (64, 256), 1)
     place = lax.broadcasted_iota(jnp.int32, (64, 256), 0)
-    qa, ka = cell // GROUP + base, cell % GROUP + base
+    qb = block_at(cell // GROUP)
+    qa, ka = qb + base, cell % GROUP + base
     code = jnp.minimum(qa, ka) * 64 + jnp.maximum(qa, ka)
     hit = (code == table[:, 1:2]) | (code == table[:, 2:3]) | (code == table[:, 3:4])
     listed = jnp.max(jnp.where(hit, 1.0, 0.0), axis=0, keepdims=True)
@@ -153,7 +164,7 @@
         preferred_element_type=jnp.float32,
     )[:1]
     pick = jnp.where((alive > 0.5) & (rank == (place + 1).astype(jnp.float32)), 1.0, 0.0)
-    cells = jnp.sum(pick * cell.astype(jnp.float32), axis=1, keepdims=True)
+    cells = jnp.sum(pick * (qb * GROUP + cell % GROUP).astype(jnp.float32), axis=1, keepdims=True)
     rank_64 = jnp.broadcast_to(rank, (64, 256))
     ends = jnp.sum(jnp.where(cell == place * GROUP + GROUP - 1, rank_64 - 1.0, 0.0), axis=1, keepdims=True)
     opens = jnp.max(
@@ -177,29 +188,22 @@
         lax.fori_loop(0, GROUP, pass_on, 0)
 
     pass_all(K, kbuf)
-    if GATE:
-        dealt(K, HALF)
-        deal_q(0)
     pass_all(V, vbuf)
-    if GATE:
-        dealt(V, HALF)
-        for u in range(1, CHUNKS):
-            deal_q(u)
+    dealt(K, HALF)
+    dealt(V, HALF)
+    deal_q(1)
     other = pl.ds(pl.multiple_of((1 - c) * HALF, HALF), HALF)
     arrived(kbuf.at[:, other], recv_sem.at[KF])
     arrived(vbuf.at[:, other], recv_sem.at[VF])
-    if not GATE:
-        dealt(K, HALF)
-        dealt(V, HALF)
     arrived(meta.at[pl.ds(0, GROUP - 1)], meta_sem.at[0])
     arrived(meta.at[pl.ds(0, 3 * GROUP)], meta_sem.at[2])
     arrived(kbuf.at[:, other], send_sem.at[KF])
 
     scale = jnp.float32(HD**-0.5 * LOG2E)
     ones = jnp.ones((BLK, HD), jnp.bfloat16)
-    columns = pl.ds(pl.multiple_of(p * HD, HD), HD)
 
     def attend(u):
+        rows = SIZES[u]
         arrived(qbuf[u], recv_sem.at[Q + u])
 
         def visit(t, carry):
@@ -216,37 +220,52 @@
             shrink = jnp.exp2((top - new_top) * scale)
             values = jnp.concatenate([vbuf[key], ones], axis=1)
             total = shrink * total + jnp.dot(weights, values, preferred_element_type=jnp.float32)
-            state[t] = total
+            state[t, pl.ds(0, rows)] = total
             return new_top, total
 
-        start = (jnp.full((ROWS, 1), -jnp.inf, jnp.float32), jnp.zeros((ROWS, 2 * HD), jnp.float32))
-        lax.fori_loop(0, TILES, visit, start, unroll=UNROLL)
-
-        def finish(n, carry):
-            b = (p + n) % GROUP
-            total = state[jnp.clip(list_s[b, 2], 0, TILES - 1)]
+        def finish(n, carry, part):
+            b = block_at(n)
+            total = state[jnp.clip(list_s[n, 2], 0, TILES - 1), pl.ds(0, rows)]
             obuf[u][b] = (total[:, :HD] / total[:, HD:]).astype(jnp.bfloat16)
-            remote(obuf[u].at[b], att[u].at[:, columns], send_sem.at[O + u], recv_sem.at[O + u], base + b, c).start()
+            dst = att.at[p, pl.ds(FIRSTS[u], rows)]
+            landed = back_sem.at[u, part]
+
+            @pl.when(b == p)
+            def _():
+                pltpu.make_async_copy(obuf[u].at[b], dst, landed).start()
+
+            @pl.when(b != p)
+            def _():
+                remote(obuf[u].at[b], dst, send_sem.at[O + u], landed, base + b, c).start()
+
             return carry
 
-        lax.fori_loop(1, GROUP, finish, 0)
-        total = state[jnp.clip(list_s[p, 2], 0, TILES - 1)]
-        obuf[u][p] = (total[:, :HD] / total[:, HD:]).astype(jnp.bfloat16)
-        pltpu.make_async_copy(obuf[u].at[p], att[u].at[:, columns], recv_sem.at[O + u]).start()
-
-    def out_copy(u):
-        return pltpu.make_async_copy(stage.at[u], out.at[pl.ds(u * ROWS, ROWS)], out_sem.at[u])
-
-    def project(u):
-        arrived(att[u], recv_sem.at[O + u])
+        now = (jnp.full((rows, 1), -jnp.inf, jnp.float32), jnp.zeros((rows, 2 * HD), jnp.float32))
+        for first, last, done_first, done_last in STEPS:
+            now = lax.fori_loop(first, last, visit, now, unroll=last - first)
+            lax.fori_loop(done_first, done_last, functools.partial(finish, part=done_first // 8), 0)
+
+    def project(part):
+        for u in range(CHUNKS):
+            arrived(att.at[pl.ds(0, 8), pl.ds(0, SIZES[u])], back_sem.at[u, part])
+        heads = [
+            (y + 4 - (STEP_Y >> 2 * m & 3) + 2 * k) % 4 * 4 + (x + 4 - (STEP_X >> 2 * m & 3)) % 4
+            for m in range(4 * part, 4 * part + 4)
+            for k in range(2)
+        ]
+        left = jnp.concatenate([att[h] for h in heads], axis=1)
 
         def tile(n, carry):
             cols = pl.ds(pl.multiple_of(n * COLS, COLS), COLS)
-            stage[u, :, cols] = jnp.dot(att[u][...], wbuf[:, cols], preferred_element_type=jnp.float32).astype(jnp.bfloat16)
+            right = jnp.concatenate([wbuf[pl.ds(pl.multiple_of(h * HD, HD), HD), cols] for h in heads], axis=0)
+            product = jnp.dot(left, right, preferred_element_type=jnp.float32)
+            if part == 0:
+                partial_sum[:, cols] = product
+            else:
+                out[:, cols] = (partial_sum[:, cols] + product).astype(jnp.bfloat16)
             return carry
 
-        lax.fori_loop(0, wbuf.shape[1] // COLS, tile, 0)
-        out_copy(u).start()
+        lax.fori_loop(0, wbuf.shape[1] // COLS, tile, 0, unroll=PROJ_UNROLL)
 
     for u in range(CHUNKS):
         attend(u)
@@ -254,13 +273,11 @@
     w_sent.wait()
     arrived(vbuf.at[:, other], send_sem.at[VF])
     for u in range(CHUNKS):
-        dealt(Q + u, ROWS)
-    for u in range(CHUNKS):
-        project(u)
+        dealt(Q + u, SIZES[u])
+    project(0)
+    project(1)
     for u in range(CHUNKS):
         arrived(obuf[u].at[pl.ds(0, GROUP - 1)], send_sem.at[O + u])
-    for u in range(CHUNKS):
-        out_copy(u).wait()
 
 
 def local(query_states, key_states, value_states, doc_ids, pair_table, out_weight):
@@ -269,29 +286,28 @@
     width = out_weight.shape[1]
     return pl.pallas_call(
         kernel,
-        out_shape=jax.ShapeDtypeStruct((HALF, width), bf16),
+        out_shape=pltpu.VMEM((HALF, width), bf16),
         in_specs=[anywhere] * 6,
-        out_specs=anywhere,
+        out_specs=pl.BlockSpec(memory_space=pltpu.VMEM),
         scratch_shapes=[
             pltpu.VMEM((GROUP, BLK, HD), bf16),
             pltpu.VMEM((GROUP, BLK, HD), bf16),
-            pltpu.VMEM((TILES, ROWS, 2 * HD), jnp.float32),
+            pltpu.VMEM((TILES, MOST, 2 * HD), jnp.float32),
             pltpu.VMEM((2048, width), bf16),
             pltpu.VMEM((64, 8, 128), jnp.int32),
             pltpu.VMEM((64, 128), jnp.int32),
             pltpu.SMEM((64, 128), jnp.int32),
             pltpu.SMEM((1,), jnp.int32),
-            pltpu.SMEM((3, 2), jnp.int32),
-            pltpu.VMEM((CHUNKS, ROWS, width), bf16),
+            pltpu.SMEM((2, 3), jnp.int32),
         ]
-        + [pltpu.VMEM((GROUP, ROWS, HD), bf16)] * CHUNKS
-        + [pltpu.VMEM((GROUP, ROWS, HD), bf16)] * CHUNKS
-        + [pltpu.VMEM((ROWS, 2048), bf16)] * CHUNKS
-        + [dma((KINDS,)), dma((KINDS,)), dma((2, GROUP)), dma((4,)), dma((3,)), dma((CHUNKS,)), dma((2,))],
+        + [pltpu.VMEM((GROUP, rows, HD), bf16) for rows in SIZES]
+        + [pltpu.VMEM((GROUP, rows, HD), bf16) for rows in SIZES]
+        + [pltpu.VMEM((GROUP, HALF, HD), bf16), pltpu.VMEM((HALF, width), jnp.float32)]
+        + [dma((KINDS,)), dma((KINDS,)), dma((CHUNKS, 2)), dma((2, GROUP)), dma((4,)), dma((3,)), dma((2,))],
         compiler_params=pltpu.CompilerParams(
             collective_id=0, has_side_effects=True, vmem_limit_bytes=56 << 20
         ),
-    )(query_states, key_states, value_states, doc_ids, pair_table, out_weight)
+    )(query_states, key_states, value_states, doc_ids, pair_table.T, out_weight)
 
 
 def solution(mesh):

time: 73.1 us -> 66.2 us (0.906)
  Pallas kernels: 67.8 us -> 64.1 us
  local copies, waits for them, and re-layouts: 4.47 us -> 1.32 us
    pallas_call x1, Pallas kernels: 67.8 us -> 64.1 us  [local(): pl.pallas_call(kernel, out_shape=pltpu.VMEM((HALF, width), bf16), in_spec...]
    unnamed x2 -> x1, local copies, waits for them, and re-layouts: 4.47 us -> 1.32 us
where the time goes in v3:
time: 66.2 us; the launch traced here: 66.1 us
  Pallas kernels  64.1 us (97%)
  local copies, waits for them, and re-layouts  1.32 us (2%)
    pallas_call x1, Pallas kernels, local(): pl.pallas_call(kernel, out_shape=pltpu.VMEM((HALF, width), bf16), in_spec...  64.1 us

profile of v3, /device:TPU:1, one launch (start us, length us, event | category | flops | bytes accessed | tf_op | source)
XLA Modules:
  0.0 66.1 jit_solution(228405339103626531)
XLA Ops:
  0.7 64.1 %shard_map.64 = bf16[256,4096]{1,0:T(8,128)(2,1)S(1)} custom-call(bf16[512,1024]{1,0:T(8,128)(2,1)} %q_in.1, bf16[512,1024]{1,0:T(8,128)(2,1)} %k_in.1, bf16[512,1024]{1,0:T(8,128)(2,1)} %v_in.1, s32[1]{0:T(128)S(6)} %copy.9.doc_in, s32[2,3]{1,0:T(2,128)} %bitcast.1, bf16[1024,4096]{1,0:T(8,128)(2,1)} %w_in.1), custom_call_target="tpu_custom_call" | custom-call | tf_op jit(solution)/shard_map/pallas_call | solution.py:287
  64.8 1.3 %copy.8 = bf16[256,4096]{1,0:T(8,128)(2,1)} copy(bf16[256,4096]{1,0:T(8,128)(2,1)S(1)} %shard_map.64) | data formatting | bytes 4194304

commit v4 on v3

--- a/solution.py
+++ b/solution.py
@@ -14,8 +14,8 @@
 TILES = 64
 SIZES = (128, 128)
 FIRSTS = (0, 128)
-STEPS = ((0, 32, 0, 4), (32, 48, 4, 8), (48, 64, 8, 16))
-PROJ_UNROLL = 4
+STEPS = ((0, 24, 0, 4), (24, 48, 4, 8), (48, 64, 8, 16))
+PROJ_UNROLL = 8
 STEP_X = sum(d << 2 * n for n, d in enumerate((2, 2, 1, 3, 1, 3, 0, 0)))
 STEP_Y = sum(d << 2 * n for n, d in enumerate((1, 0, 1, 1, 0, 0, 1, 0)))
 CHUNKS = len(SIZES)
@@ -99,7 +99,7 @@
 
     def deal(kind, ref, dst, recv, first_row, rows):
         def step(n, carry):
-            i = (n + p) % 8
+            i = (5 * n + p + 2) % 8
             seq = base + 8 * c + i
             for j in range(2):
                 src = ref.at[pl.ds(j * HALF + first_row, rows), pl.ds(pl.multiple_of(i * HD, HD), HD)]
@@ -139,6 +139,7 @@
     w_sent = remote(w_in, wbuf.at[w_rows], w_sem.at[1], w_sem.at[2], s, 1 - c)
     w_sent.start()
     deal_q(0)
+    deal_q(1)
 
     arrived(meta.at[pl.ds(0, GROUP - 1)], meta_sem.at[1])
     lax.fori_loop(1, 4, far_copy, 0)
@@ -191,7 +192,6 @@
     pass_all(V, vbuf)
     dealt(K, HALF)
     dealt(V, HALF)
-    deal_q(1)
     other = pl.ds(pl.multiple_of((1 - c) * HALF, HALF), HALF)
     arrived(kbuf.at[:, other], recv_sem.at[KF])
     arrived(vbuf.at[:, other], recv_sem.at[VF])

time: 66.2 us -> 63.8 us (0.964)
  Pallas kernels: 64.1 us -> 61.7 us
    pallas_call x1, Pallas kernels: 64.1 us -> 61.7 us  [local(): pl.pallas_call(kernel, out_shape=pltpu.VMEM((HALF, width), bf16), in_spec...]
where the time goes in v4:
time: 63.8 us; the launch traced here: 63.7 us
  Pallas kernels  61.7 us (97%)
  local copies, waits for them, and re-layouts  1.32 us (2%)
  between operations  0.66 us (1%)
    pallas_call x1, Pallas kernels, local(): pl.pallas_call(kernel, out_shape=pltpu.VMEM((HALF, width), bf16), in_spec...  61.7 us
    unnamed x1, local copies, waits for them, and re-layouts  1.32 us

profile of v4, /device:TPU:1, one launch (start us, length us, event | category | flops | bytes accessed | tf_op | source)
XLA Modules:
  0.0 63.7 jit_solution(9325311673099461222)
XLA Ops:
  0.7 61.7 %shard_map.64 = bf16[256,4096]{1,0:T(8,128)(2,1)S(1)} custom-call(bf16[512,1024]{1,0:T(8,128)(2,1)} %q_in.1, bf16[512,1024]{1,0:T(8,128)(2,1)} %k_in.1, bf16[512,1024]{1,0:T(8,128)(2,1)} %v_in.1, s32[1]{0:T(128)S(6)} %copy.9.doc_in, s32[2,3]{1,0:T(2,128)} %bitcast.1, bf16[1024,4096]{1,0:T(8,128)(2,1)} %w_in.1), custom_call_target="tpu_custom_call" | custom-call | tf_op jit(solution)/shard_map/pallas_call | solution.py:287
  62.3 1.3 %copy.8 = bf16[256,4096]{1,0:T(8,128)(2,1)} copy(bf16[256,4096]{1,0:T(8,128)(2,1)S(1)} %shard_map.64) | data formatting | bytes 4194304

commit v5 on v4

--- a/solution.py
+++ b/solution.py
@@ -223,10 +223,14 @@
             state[t, pl.ds(0, rows)] = total
             return new_top, total
 
-        def finish(n, carry, part):
+        def finish(n, carry):
             b = block_at(n)
             total = state[jnp.clip(list_s[n, 2], 0, TILES - 1), pl.ds(0, rows)]
             obuf[u][b] = (total[:, :HD] / total[:, HD:]).astype(jnp.bfloat16)
+            return carry
+
+        def send(n, carry, part):
+            b = block_at(n)
             dst = att.at[p, pl.ds(FIRSTS[u], rows)]
             landed = back_sem.at[u, part]
 
@@ -243,7 +247,8 @@
         now = (jnp.full((rows, 1), -jnp.inf, jnp.float32), jnp.zeros((rows, 2 * HD), jnp.float32))
         for first, last, done_first, done_last in STEPS:
             now = lax.fori_loop(first, last, visit, now, unroll=last - first)
-            lax.fori_loop(done_first, done_last, functools.partial(finish, part=done_first // 8), 0)
+            lax.fori_loop(done_first, done_last, finish, 0, unroll=4)
+            lax.fori_loop(done_first, done_last, functools.partial(send, part=done_first // 8), 0)
 
     def project(part):
         for u in range(CHUNKS):

time: 63.8 us -> 63.7 us (level)
  no operation moved by 1% of the time
where the time goes in v5:
time: 63.7 us; the launch traced here: 63.6 us
  Pallas kernels  61.6 us (97%)
  local copies, waits for them, and re-layouts  1.32 us (2%)
  between operations  0.66 us (1%)
    pallas_call x1, Pallas kernels, local(): pl.pallas_call(kernel, out_shape=pltpu.VMEM((HALF, width), bf16), in_spec...  61.6 us
    unnamed x1, local copies, waits for them, and re-layouts  1.32 us

profile of v5, /device:TPU:1, one launch (start us, length us, event | category | flops | bytes accessed | tf_op | source)
XLA Modules:
  0.0 63.6 jit_solution(12377371458767599145)
XLA Ops:
  0.7 61.6 %shard_map.64 = bf16[256,4096]{1,0:T(8,128)(2,1)S(1)} custom-call(bf16[512,1024]{1,0:T(8,128)(2,1)} %q_in.1, bf16[512,1024]{1,0:T(8,128)(2,1)} %k_in.1, bf16[512,1024]{1,0:T(8,128)(2,1)} %v_in.1, s32[1]{0:T(128)S(6)} %copy.9.doc_in, s32[2,3]{1,0:T(2,128)} %bitcast.1, bf16[1024,4096]{1,0:T(8,128)(2,1)} %w_in.1), custom_call_target="tpu_custom_call" | custom-call | tf_op jit(solution)/shard_map/pallas_call | solution.py:292
  62.3 1.3 %copy.8 = bf16[256,4096]{1,0:T(8,128)(2,1)} copy(bf16[256,4096]{1,0:T(8,128)(2,1)S(1)} %shard_map.64) | data formatting | bytes 4194304
